TPU v7x, 32 devices: a whole 2x2x4 slice. The times are simulated.
32 devices in a mesh: gx: 8 (over y, x, core), gy: 4 (over z).
Axes of the slice: x: 2, y: 2, z: 4, core: 2. Of those that a mesh axis runs over, the one named last changes fastest.
Arguments:
- provisional: bfloat16 [4, 8, 1024, 1024], P(None, 'gx', 'gy'), may hold values from -6 to 6
- implicit_terms: bfloat16 [4, 8, 1024, 1024], P(None, 'gx', 'gy'), may hold values from -6 to 6
- adv_speed: float32 [8, 1024], P('gx'), may hold values from 0.2 to 1.2
- reaction: float32 [8, 1024], P('gx'), may hold values from 0.1 to 2
- wall_rate: float32 [1024], replicated, may hold values from 0.05 to 20
- span_rate: float32 [1024], replicated, may hold values from 0.01 to 4
- analysis: bfloat16 [1024, 1024], replicated, may hold values from -1 to 2
- synthesis: bfloat16 [1024, 1024], replicated, may hold values from -1 to 2
Outputs:
- end_value: float32 [8, 1024, 1024], P('gx', 'gy')
All inputs are finite; a program needn't handle non-finite values.
Results may differ from a plain program's by a relative error of at most 0.0063.
Values may be sent and summed in bfloat16 or wider, within the bound.
A program may use at most 64 MiB of HBM per device.

v0:
```python
import math
import jax
import jax.numpy as jnp
from jax import lax
from jax.sharding import PartitionSpec as P


def extended(cells, sides, width):
    for axis, dim in sides:
        count = lax.axis_size(axis)
        head = lax.slice_in_dim(cells, 0, width, axis=dim)
        tail = lax.slice_in_dim(cells, cells.shape[dim] - width, cells.shape[dim], axis=dim)
        cells = jnp.concatenate(
            [
                lax.ppermute(tail, axis, [(i, (i + 1) % count) for i in range(count)]),
                cells,
                lax.ppermute(head, axis, [((i + 1) % count, i) for i in range(count)]),
            ],
            axis=dim,
        )
    return cells


def spectral_weights():
    root_five = math.sqrt(5.0)
    points = [0.0, 0.5 - 0.5 / root_five, 0.5 + 0.5 / root_five, 1.0]
    gauss_offset = 1.0 / math.sqrt(3.0)
    weights = [[0.0, 0.0, 0.0, 0.0] for m in range(3)]
    for m in range(3):
        half_width = 0.5 * (points[m + 1] - points[m])
        centre = 0.5 * (points[m + 1] + points[m])
        for sign_factor in (-1.0, 1.0):
            sample = centre + half_width * sign_factor * gauss_offset
            for j in range(4):
                basis_value = 1.0
                for i in range(4):
                    if i != j:
                        basis_value = basis_value * (sample - points[i]) / (points[j] - points[i])
                weights[m][j] = weights[m][j] + half_width * basis_value
    return (points, weights)


def explicit_term(values, velocity, decay_rate):
    padded = extended(values, (("gx", 1),), 1)
    forward = padded[:, 2:].astype(jnp.float32)
    behind = padded[:, :-2].astype(jnp.float32)
    return -velocity * (forward - behind) * 0.5 - decay_rate * values.astype(jnp.float32)


def wall_solve(rhs_block, analysis, synthesis, factors):
    coefficients = jnp.einsum(
        "ij,xjk->xik", analysis, rhs_block, preferred_element_type=jnp.float32
    )
    scaled = (coefficients * factors).astype(jnp.bfloat16)
    return jnp.einsum("ji,xik->xjk", synthesis, scaled, preferred_element_type=jnp.float32)


def per_device(
    provisional, implicit_terms, adv_speed, reaction, wall_rate, span_rate, analysis, synthesis
):
    points, weights = spectral_weights()
    modes_dev = span_rate.shape[0] // lax.axis_size("gy")
    span_part = lax.dynamic_slice_in_dim(span_rate, lax.axis_index("gy") * modes_dev, modes_dev, 0)
    rows_dev = provisional.shape[2]
    row_start = lax.axis_index("gy") * rows_dev
    velocity = lax.dynamic_slice_in_dim(adv_speed, row_start, rows_dev, 1)[None, :, :, None]
    decay_rate = lax.dynamic_slice_in_dim(reaction, row_start, rows_dev, 1)[None, :, :, None]
    old_explicit = explicit_term(provisional, velocity, decay_rate)
    sources = old_explicit + implicit_terms.astype(jnp.float32)
    current = provisional[0].astype(jnp.float32)
    new_explicit = old_explicit[0]
    for m in range(3):
        step_size = float(points[m + 1] - points[m])
        quadrature = float(weights[m][0]) * sources[0]
        for j in range(1, 4):
            quadrature = quadrature + float(weights[m][j]) * sources[j]
        rhs = (
            current
            + step_size * (new_explicit - old_explicit[m])
            - step_size * implicit_terms[m + 1].astype(jnp.float32)
            + quadrature
        )
        rounded = rhs.astype(jnp.bfloat16)
        factors = 1.0 / (1.0 + step_size * (wall_rate[:, None] + span_part[None, :]))
        solved = wall_solve(
            lax.all_to_all(rounded, "gy", split_axis=2, concat_axis=1, tiled=True),
            analysis,
            synthesis,
            factors,
        )
        current = lax.all_to_all(solved, "gy", split_axis=1, concat_axis=2, tiled=True)
        if m < 2:
            new_explicit = explicit_term(current.astype(jnp.bfloat16)[None], velocity, decay_rate)[
                0
            ]
    return current


def solution(mesh):
    placed = (
        P(None, "gx", "gy", None),
        P(None, "gx", "gy", None),
        P("gx", None),
        P("gx", None),
        P(),
        P(),
        P(),
        P(),
    )
    return jax.shard_map(
        per_device, mesh=mesh, in_specs=placed, out_specs=P("gx", "gy", None), check_vma=False
    )
```

profile of v0, /device:TPU:0, one launch (start us, length us, event | category | flops | bytes accessed | tf_op | source)
XLA Modules:
  0.0 308.2 jit_solution(4075768437817554544)
XLA Ops:
  0.0 0.0 copy-start
  0.0 3.3 %collective-permute-start = (bf16[4,1,256,1024]{3,2,1,0:T(8,128)(2,1)}, bf16[4,1,256,1024]{3,2,1,0:T(8,128)(2,1)}, u32[]{:S(2)}, u32[]{:S(2)}) collective-permute-start(bf16[4,1,256,1024]{3,2,1,0:T(8,128)(2,1)} %param.8), channel_id=1, source_target_pairs={{4,0},{8,4},{12,8},{16,12},{20,16},{24,20},{28,24},{0,28},{5,1},{9... | collective-permute-start | bytes 6291464 | tf_op jit(solution)/shard_map/ppermute | solution.py:17
  3.3 0.0 collective-permute-start.1
  3.3 0.7 dynamic-slice_negate_fusion
  4.0 44.7 %collective-permute-done = bf16[4,1,256,1024]{3,2,1,0:T(8,128)(2,1)} collective-permute-done((bf16[4,1,256,1024]{3,2,1,0:T(8,128)(2,1)}, bf16[4,1,256,1024]{3,2,1,0:T(8,128)(2,1)}, u32[]{:S(2)}, u32[]{:S(2)}) %collective-permute-start) | collective-permute-done | bytes 2097184 | tf_op jit(solution)/shard_map/ppermute | solution.py:17
  48.8 1.9 collective-permute-done.1
  50.7 5.7 %convert_add_fusion = (f32[4,1,256,1024]{3,2,1,0:T(8,128)S(1)}, f32[4,1,256,1024]{3,2,1,0:T(8,128)S(1)}) fusion(bf16[4,1,256,1024]{3,2,1,0:T(8,128)(2,1)} %param.9, bf16[4,1,256,1024]{3,2,1,0:T(8,128)(2,1)} %param.8, f32[256]{0:T(256)S(1)} %bitcast.160, bf16[4,1,256,1024]{3,2,1,0:T(8,128)(2,1)} %collective-permute-done.1, ...), kind=kLoop, calls=%fused_computation | loop fusion | flops 10485760 | bytes 16779264 | tf_op jit(solution)/shard_map/add | solution.py:69
  56.4 0.0 copy-start.1
  56.4 2.0 copy-done.1
  58.4 1.2 copy-done.2
  59.6 2.8 fusion.42
  62.3 2.4 copy.54
  64.7 0.5 broadcast.416
  65.2 4.5 %reduce = bf16[1024,256]{1,0:T(8,128)(2,1)} reduce(bf16[1024,1,256]{2,1,0:T(2,128)(2,1)S(1)} %bitcast.143, bf16[]{:T(256)} %broadcast.416), dimensions={1}, to_apply=%bitcast.117.reduce_sub_computation | reduce | bytes 1048578
  69.8 2.0 reshape.671
  71.8 4.9 %all-to-all-start = ((bf16[4,2,32768]{2,1,0:T(2,128)(2,1)}), bf16[4,2,32768]{2,1,0:T(2,128)(2,1)}, u32[]{:S(2)}, u32[]{:S(2)}) async-start(bf16[4,2,32768]{2,1,0:T(2,128)(2,1)} %reshape.671), calls=%async_computation | async-start | bytes 1048576 | tf_op jit(solution)/shard_map/all_to_all | solution.py:86
  76.6 0.8 dynamic_slice.11
  77.4 11.3 %all-to-all-done = bf16[4,2,32768]{2,1,0:T(2,128)(2,1)} async-done(((bf16[4,2,32768]{2,1,0:T(2,128)(2,1)}), bf16[4,2,32768]{2,1,0:T(2,128)(2,1)}, u32[]{:S(2)}, u32[]{:S(2)}) %all-to-all-start) | async-done | bytes 524320 | tf_op jit(solution)/shard_map/all_to_all | solution.py:86
  88.7 2.2 reshape.672
  90.9 0.9 copy.66
  91.8 2.1 copy.55
  93.9 3.2 %convolution_bitcast_fusion.4 = f32[1,1024,256]{1,2,0:T(8,128)S(1)} fusion(bf16[1024,1024]{1,0:T(8,128)(2,1)S(1)} %copy-done, bf16[1024,256]{1,0:T(8,128)(2,1)} %bitcast.155, bf16[1024,1024]{1,0:T(8,128)(2,1)} %param.14, f32[256]{0:T(256)S(1)} %dynamic_slice.11, f32[1024]{0:T(1024)S(1)} %copy-done.3), kind=kOutput, calls=%fused_computation.8 | convolution fusion | flops 1075314688 | bytes 5772288 | tf_op jit(solution)/shard_map/ji,xik->xjk/dot_general | solution.py:55
  97.1 1.9 copy.56
  99.0 27.0 %all_to_all.99 = f32[1,1024,256]{2,0,1:T(1,128)S(1)} all-to-all(f32[1,1024,256]{2,0,1:T(1,128)} %copy.56), channel_id=1, replica_groups=mesh['gx'=8,'gy'=4] {'gy'}, dimensions={1} | all-to-all | bytes 2097152 | tf_op jit(solution)/shard_map/all_to_all | solution.py:91
  125.9 1.5 copy.77
  127.4 2.2 convert_element_type.185
  129.6 4.0 %collective-permute-start.2 = (bf16[1,1,256,1024]{3,2,1,0:T(8,128)(2,1)}, bf16[1,1,256,1024]{3,2,1,0:T(8,128)(2,1)}, u32[]{:S(2)}, u32[]{:S(2)}) collective-permute-start(bf16[1,1,256,1024]{3,2,1,0:T(8,128)(2,1)} %convert_element_type.185), channel_id=1, source_target_pairs={{4,0},{8,4},{12,8},{16,12},{20,16},{24,20},{28,24},{0,28},{5,1},{9... | collective-permute-start | bytes 1572872 | tf_op jit(solution)/shard_map/ppermute | solution.py:17
  133.6 0.0 collective-permute-start.3
  133.6 1.6 copy.76
  135.2 1.8 all_to_all.78
  137.0 7.5 %collective-permute-done.2 = bf16[1,1,256,1024]{3,2,1,0:T(8,128)(2,1)} collective-permute-done((bf16[1,1,256,1024]{3,2,1,0:T(8,128)(2,1)}, bf16[1,1,256,1024]{3,2,1,0:T(8,128)(2,1)}, u32[]{:S(2)}, u32[]{:S(2)}) %collective-permute-start.2) | collective-permute-done | bytes 524320 | tf_op jit(solution)/shard_map/ppermute | solution.py:17
  144.5 4.0 %collective-permute-done.3 = bf16[1,1,256,1024]{3,2,1,0:T(8,128)(2,1)} collective-permute-done((bf16[1,1,256,1024]{3,2,1,0:T(8,128)(2,1)}, bf16[1,1,256,1024]{3,2,1,0:T(8,128)(2,1)}, u32[]{:S(2)}, u32[]{:S(2)}) %collective-permute-start.3) | collective-permute-done | bytes 524320 | tf_op jit(solution)/shard_map/ppermute | solution.py:15
  148.5 4.9 %fusion.24 = bf16[1,256,1024]{2,1,0:T(8,128)(2,1)} fusion(f32[1,256,1024]{2,1,0:T(8,128)S(1)} %all_to_all.78, f32[4,1,256,1024]{3,2,1,0:T(8,128)} %copy-done.2, bf16[1,1,256,1024]{3,2,1,0:T(8,128)(2,1)} %convert_element_type.185, bf16[1,1,256,1024]{3,2,1,0:T(8,128)(2,1)} %collective-permute-done.3, bf16[1,1,256,1024]{3,2,1,0:T(8,128)(2,1)} %collective-permute-done.2, ...), kind=kLoop, calls=%fused_computation.36 | loop fusion | flops 6029312 | bytes 8914944 | tf_op jit(solution)/shard_map/convert_element_type | solution.py:83
  153.3 2.4 copy.58
  155.7 4.5 %reduce.1 = bf16[1024,256]{1,0:T(8,128)(2,1)} reduce(bf16[1024,1,256]{2,1,0:T(2,128)(2,1)S(1)} %bitcast.146, bf16[]{:T(256)} %broadcast.416), dimensions={1}, to_apply=%bitcast.119.reduce_sub_computation | reduce | bytes 1048578
  160.3 1.2 reshape.673
  161.4 17.3 %all_to_all.100 = bf16[4,2,32768]{2,1,0:T(2,128)(2,1)} all-to-all(bf16[4,2,32768]{2,1,0:T(2,128)(2,1)S(1)} %reshape.673), channel_id=1, replica_groups=mesh['gx'=8,'gy'=4] {'gy'}, dimensions={0} | all-to-all | bytes 1048576 | tf_op jit(solution)/shard_map/all_to_all | solution.py:86
  178.7 2.2 reshape.674
  181.0 0.9 copy.67
  181.8 2.1 copy.59
  183.9 3.2 %convolution_bitcast_fusion.2 = f32[1,1024,256]{1,2,0:T(8,128)S(1)} fusion(bf16[1024,1024]{1,0:T(8,128)(2,1)S(1)} %copy-done, bf16[1024,256]{1,0:T(8,128)(2,1)} %bitcast.156, bf16[1024,1024]{1,0:T(8,128)(2,1)} %param.14, f32[256]{0:T(256)S(1)} %dynamic_slice.11, f32[1024]{0:T(1024)S(1)} %copy-done.3), kind=kOutput, calls=%fused_computation.6 | convolution fusion | flops 1075314688 | bytes 5772288 | tf_op jit(solution)/shard_map/ji,xik->xjk/dot_general | solution.py:55
  187.1 1.9 copy.60
  189.0 28.3 %all_to_all.101 = f32[1,1024,256]{2,0,1:T(1,128)S(1)} all-to-all(f32[1,1024,256]{2,0,1:T(1,128)} %copy.60), channel_id=1, replica_groups=mesh['gx'=8,'gy'=4] {'gy'}, dimensions={1} | all-to-all | bytes 2097152 | tf_op jit(solution)/shard_map/all_to_all | solution.py:91
  217.3 1.5 copy.78
  218.7 2.2 convert_element_type.193
  221.0 0.0 collective-permute-start.4
  221.0 0.5 collective-permute-start.5
  221.5 1.6 copy.75
  223.1 1.8 all_to_all.85
  224.9 6.0 %collective-permute-done.4 = bf16[1,1,256,1024]{3,2,1,0:T(8,128)(2,1)} collective-permute-done((bf16[1,1,256,1024]{3,2,1,0:T(8,128)(2,1)}, bf16[1,1,256,1024]{3,2,1,0:T(8,128)(2,1)}, u32[]{:S(2)}, u32[]{:S(2)}) %collective-permute-start.4) | collective-permute-done | bytes 524320 | tf_op jit(solution)/shard_map/ppermute | solution.py:17
  230.9 3.9 %collective-permute-done.5 = bf16[1,1,256,1024]{3,2,1,0:T(8,128)(2,1)} collective-permute-done((bf16[1,1,256,1024]{3,2,1,0:T(8,128)(2,1)}, bf16[1,1,256,1024]{3,2,1,0:T(8,128)(2,1)}, u32[]{:S(2)}, u32[]{:S(2)}) %collective-permute-start.5) | collective-permute-done | bytes 524320 | tf_op jit(solution)/shard_map/ppermute | solution.py:15
  234.8 4.9 %fusion.18 = bf16[1,256,1024]{2,1,0:T(8,128)(2,1)} fusion(f32[1,256,1024]{2,1,0:T(8,128)S(1)} %all_to_all.85, f32[4,1,256,1024]{3,2,1,0:T(8,128)} %copy-done.2, bf16[1,1,256,1024]{3,2,1,0:T(8,128)(2,1)} %convert_element_type.193, bf16[1,1,256,1024]{3,2,1,0:T(8,128)(2,1)} %collective-permute-done.5, bf16[1,1,256,1024]{3,2,1,0:T(8,128)(2,1)} %collective-permute-done.4, ...), kind=kLoop, calls=%fused_computation.29 | loop fusion | flops 6029312 | bytes 8914944 | tf_op jit(solution)/shard_map/convert_element_type | solution.py:83
  239.7 2.4 copy.62
  242.1 4.5 %reduce.2 = bf16[1024,256]{1,0:T(8,128)(2,1)} reduce(bf16[1024,1,256]{2,1,0:T(2,128)(2,1)S(1)} %bitcast.144, bf16[]{:T(256)} %broadcast.416), dimensions={1}, to_apply=%bitcast.121.reduce_sub_computation | reduce | bytes 1048578
  246.6 1.2 reshape.675
  247.8 18.7 %all_to_all.102 = bf16[4,2,32768]{2,1,0:T(2,128)(2,1)} all-to-all(bf16[4,2,32768]{2,1,0:T(2,128)(2,1)S(1)} %reshape.675), channel_id=1, replica_groups=mesh['gx'=8,'gy'=4] {'gy'}, dimensions={0} | all-to-all | bytes 1048576 | tf_op jit(solution)/shard_map/all_to_all | solution.py:86
  266.5 2.2 reshape.676
  268.7 0.9 copy.68
  269.6 1.2 copy.63
  270.9 4.0 %convolution_bitcast_fusion = f32[1,1024,256]{1,2,0:T(8,128)} fusion(bf16[1024,1024]{1,0:T(8,128)(2,1)S(1)} %copy-done, bf16[1024,256]{1,0:T(8,128)(2,1)S(1)} %bitcast.154, bf16[1024,1024]{1,0:T(8,128)(2,1)} %param.14, f32[256]{0:T(256)S(1)} %dynamic_slice.11, f32[1024]{0:T(1024)S(1)} %copy-done.3), kind=kOutput, calls=%fused_computation.4 | convolution fusion | flops 1075314688 | bytes 5772288 | tf_op jit(solution)/shard_map/ji,xik->xjk/dot_general | solution.py:55
  274.9 2.4 copy.64
  277.3 28.7 %all_to_all.103 = f32[1,1024,256]{2,0,1:T(1,128)S(1)} all-to-all(f32[1,1024,256]{2,0,1:T(1,128)S(1)} %copy.64), channel_id=1, replica_groups=mesh['gx'=8,'gy'=4] {'gy'}, dimensions={1} | all-to-all | bytes 2097152 | tf_op jit(solution)/shard_map/all_to_all | solution.py:91
  306.0 0.7 copy.65
  306.7 1.5 all_to_all.92
  (4 shorter events, 0.0 us)
Async XLA Ops:
  0.0 93.9 %copy-start = (bf16[1024,1024]{1,0:T(8,128)(2,1)S(1)}, bf16[1024,1024]{1,0:T(8,128)(2,1)}, u32[]{:S(2)}) copy-start(bf16[1024,1024]{1,0:T(8,128)(2,1)} %param.15) | copy-start | bytes 6291460
  0.0 48.8 %collective-permute-start = (bf16[4,1,256,1024]{3,2,1,0:T(8,128)(2,1)}, bf16[4,1,256,1024]{3,2,1,0:T(8,128)(2,1)}, u32[]{:S(2)}, u32[]{:S(2)}) collective-permute-start(bf16[4,1,256,1024]{3,2,1,0:T(8,128)(2,1)} %param.8), channel_id=1, source_target_pairs={{4,0},{8,4},{12,8},{16,12},{20,16},{24,20},{28,24},{0,28},{5,1},{9... | collective-permute-start | bytes 6291464 | tf_op jit(solution)/shard_map/ppermute | solution.py:17
  3.3 47.4 %collective-permute-start.1 = (bf16[4,1,256,1024]{3,2,1,0:T(8,128)(2,1)}, bf16[4,1,256,1024]{3,2,1,0:T(8,128)(2,1)}, u32[]{:S(2)}, u32[]{:S(2)}) collective-permute-start(bf16[4,1,256,1024]{3,2,1,0:T(8,128)(2,1)} %param.8), channel_id=1, source_target_pairs={{0,4},{4,8},{8,12},{12,16},{16,20},{20,24},{24,28},{28,0},{1,5},{5... | collective-permute-start | bytes 6291464 | tf_op jit(solution)/shard_map/ppermute | solution.py:15
  56.4 2.0 copy-start.1
  56.4 3.2 %copy-start.2 = (f32[4,1,256,1024]{3,2,1,0:T(8,128)}, f32[4,1,256,1024]{3,2,1,0:T(8,128)S(1)}, u32[]{:S(2)}) copy-start(f32[4,1,256,1024]{3,2,1,0:T(8,128)S(1)} %get-tuple-element.6) | copy-start | bytes 12582916
  71.8 16.9 %all-to-all-start = ((bf16[4,2,32768]{2,1,0:T(2,128)(2,1)}), bf16[4,2,32768]{2,1,0:T(2,128)(2,1)}, u32[]{:S(2)}, u32[]{:S(2)}) async-start(bf16[4,2,32768]{2,1,0:T(2,128)(2,1)} %reshape.671), calls=%async_computation | async-start | bytes 1048576 | tf_op jit(solution)/shard_map/all_to_all | solution.py:86
  77.4 16.5 %copy-start.3 = (f32[1024]{0:T(1024)S(1)}, f32[1024]{0:T(1024)}, u32[]{:S(2)}) copy-start(f32[1024]{0:T(1024)} %param.12) | copy-start | bytes 12292
  129.6 14.9 %collective-permute-start.2 = (bf16[1,1,256,1024]{3,2,1,0:T(8,128)(2,1)}, bf16[1,1,256,1024]{3,2,1,0:T(8,128)(2,1)}, u32[]{:S(2)}, u32[]{:S(2)}) collective-permute-start(bf16[1,1,256,1024]{3,2,1,0:T(8,128)(2,1)} %convert_element_type.185), channel_id=1, source_target_pairs={{4,0},{8,4},{12,8},{16,12},{20,16},{24,20},{28,24},{0,28},{5,1},{9... | collective-permute-start | bytes 1572872 | tf_op jit(solution)/shard_map/ppermute | solution.py:17
  133.6 14.9 %collective-permute-start.3 = (bf16[1,1,256,1024]{3,2,1,0:T(8,128)(2,1)}, bf16[1,1,256,1024]{3,2,1,0:T(8,128)(2,1)}, u32[]{:S(2)}, u32[]{:S(2)}) collective-permute-start(bf16[1,1,256,1024]{3,2,1,0:T(8,128)(2,1)} %convert_element_type.185), channel_id=1, source_target_pairs={{0,4},{4,8},{8,12},{12,16},{16,20},{20,24},{24,28},{28,0},{1,5},{5... | collective-permute-start | bytes 1572872 | tf_op jit(solution)/shard_map/ppermute | solution.py:15
  221.0 9.9 %collective-permute-start.4 = (bf16[1,1,256,1024]{3,2,1,0:T(8,128)(2,1)}, bf16[1,1,256,1024]{3,2,1,0:T(8,128)(2,1)}, u32[]{:S(2)}, u32[]{:S(2)}) collective-permute-start(bf16[1,1,256,1024]{3,2,1,0:T(8,128)(2,1)} %convert_element_type.193), channel_id=1, source_target_pairs={{4,0},{8,4},{12,8},{16,12},{20,16},{24,20},{28,24},{0,28},{5,1},{9... | collective-permute-start | bytes 1572872 | tf_op jit(solution)/shard_map/ppermute | solution.py:17
  221.0 13.8 %collective-permute-start.5 = (bf16[1,1,256,1024]{3,2,1,0:T(8,128)(2,1)}, bf16[1,1,256,1024]{3,2,1,0:T(8,128)(2,1)}, u32[]{:S(2)}, u32[]{:S(2)}) collective-permute-start(bf16[1,1,256,1024]{3,2,1,0:T(8,128)(2,1)} %convert_element_type.193), channel_id=1, source_target_pairs={{0,4},{4,8},{8,12},{12,16},{16,20},{20,24},{24,28},{28,0},{1,5},{5... | collective-permute-start | bytes 1572872 | tf_op jit(solution)/shard_map/ppermute | solution.py:15
where the time goes:
time: 310 us; the launch traced here: 308 us
  blocking collectives  120 us (39%)
  waiting for transfers between devices  79.3 us (26%)
  local copies, waits for them, and re-layouts  53.3 us (17%)
  other arithmetic  32.4 us (10%)
  starting transfers between devices  12.7 us (4%)
  matrix products  10.4 us (3%)
    all_to_all x3, blocking collectives, per_device(): lax.all_to_all(solved, 'gy', split_axis=1, concat_axis=2, tiled=True)  83.9 us
    ppermute x3, waiting for transfers between devices, extended(): lax.ppermute(head, axis, [((i + 1) % count, i) for i in range(count)])  58.2 us
    all_to_all x2, blocking collectives, per_device(): lax.all_to_all(rounded, 'gy', split_axis=2, concat_axis=1, tiled=True)  36 us
    unnamed x18, local copies, waits for them, and re-layouts  17.3 us
    unnamed x3, other arithmetic  13.6 us
    convert_element_type x3, other arithmetic, per_device(): rounded = rhs.astype(jnp.bfloat16)  12.5 us
    all_to_all x8, local copies, waits for them, and re-layouts, per_device(): lax.all_to_all(solved, 'gy', split_axis=1, concat_axis=2, tiled=True)  11.9 us
    all_to_all x1, waiting for transfers between devices, per_device(): lax.all_to_all(rounded, 'gy', split_axis=2, concat_axis=1, tiled=True)  11.3 us
  transfers between devices with their start and end apart: 7, of which 7 were waited for; matrix products, arithmetic and copies ran while one was open for 2% of the time, Pallas kernels for 0%

commit v1 on v0

--- a/solution.py
+++ b/solution.py
@@ -3,6 +3,22 @@
 import jax.numpy as jnp
 from jax import lax
 from jax.sharding import PartitionSpec as P
+
+
+def touch_gates(view, a_name="gy"):
+    taken_in, current_block = (jax.lax.axis_size(a_name), jax.lax.axis_index(a_name))
+    x_new = view.shape[2] // taken_in
+    earlier = list(view.shape)
+    earlier[2] = x_new
+    o_now = earlier[1]
+    earlier[1] = o_now * taken_in
+    main = jnp.zeros(earlier, view.dtype)
+    for tick in range(taken_in):
+        heard = lax.dynamic_slice_in_dim(view, (current_block ^ tick) * x_new, x_new, axis=2)
+        if tick:
+            heard = jax.lax.ppermute(heard, a_name, [(k, k ^ tick) for k in range(taken_in)])
+        main = lax.dynamic_update_slice_in_dim(main, heard, (current_block ^ tick) * o_now, axis=1)
+    return main
 
 
 def extended(cells, sides, width):
@@ -82,12 +98,7 @@
         )
         rounded = rhs.astype(jnp.bfloat16)
         factors = 1.0 / (1.0 + step_size * (wall_rate[:, None] + span_part[None, :]))
-        solved = wall_solve(
-            lax.all_to_all(rounded, "gy", split_axis=2, concat_axis=1, tiled=True),
-            analysis,
-            synthesis,
-            factors,
-        )
+        solved = wall_solve(touch_gates(rounded), analysis, synthesis, factors)
         current = lax.all_to_all(solved, "gy", split_axis=1, concat_axis=2, tiled=True)
         if m < 2:
             new_explicit = explicit_term(current.astype(jnp.bfloat16)[None], velocity, decay_rate)[

time: 310 us -> 255 us (0.82)
  blocking collectives: 120 us -> 85.1 us
  local copies, waits for them, and re-layouts: 53.3 us -> 31.1 us
  other arithmetic: 32.4 us -> 18.8 us
  waiting for transfers between devices: 79.3 us -> 88.1 us
  starting transfers between devices: 12.7 us -> 20.8 us
    all_to_all x2 -> x0, blocking collectives: 36 us -> none  [per_device(): lax.all_to_all(rounded, 'gy', split_axis=2, concat_axis=1, tiled=True)]
    ppermute x0 -> x9, waiting for transfers between devices: none -> 20.4 us  [touch_gates(): jax.lax.ppermute(heard, a_name, [(k, k ^ tick) for k in range(taken_in)])]
    unnamed x18 -> x8, local copies, waits for them, and re-layouts: 17.3 us -> 0.38 us
    unnamed x3 -> x0, other arithmetic: 13.6 us -> none
    ppermute x0 -> x9, starting transfers between devices: none -> 13.3 us  [touch_gates(): jax.lax.ppermute(heard, a_name, [(k, k ^ tick) for k in range(taken_in)])]
    all_to_all x1 -> x0, waiting for transfers between devices: 11.3 us -> none  [per_device(): lax.all_to_all(rounded, 'gy', split_axis=2, concat_axis=1, tiled=True)]
    convert_element_type x3 -> x0, local copies, waits for them, and re-layouts: 7.18 us -> none  [per_device(): rounded = rhs.astype(jnp.bfloat16)]
    all_to_all x3 -> x0, local copies, waits for them, and re-layouts: 5.41 us -> none  [per_device(): lax.all_to_all(rounded, 'gy', split_axis=2, concat_axis=1, tiled=True)]
  transfers between devices with their start and end apart: 7 -> 15, of which waited for: 7 -> 11; matrix products, arithmetic and copies ran while one was open for 2% -> 4% of each run, Pallas kernels for 0% -> 0%
where the time goes in v1:
time: 255 us; the launch traced here: 254 us
  waiting for transfers between devices  88.1 us (35%)
  blocking collectives  85.1 us (33%)
  local copies, waits for them, and re-layouts  31.1 us (12%)
  starting transfers between devices  20.8 us (8%)
  other arithmetic  18.8 us (7%)
  matrix products  10.4 us (4%)
    all_to_all x3, blocking collectives, per_device(): lax.all_to_all(solved, 'gy', split_axis=1, concat_axis=2, tiled=True)  85.1 us
    ppermute x3, waiting for transfers between devices, extended(): lax.ppermute(head, axis, [((i + 1) % count, i) for i in range(count)])  58.9 us
    ppermute x9, waiting for transfers between devices, touch_gates(): jax.lax.ppermute(heard, a_name, [(k, k ^ tick) for k in range(taken_in)])  20.4 us
    ppermute x9, starting transfers between devices, touch_gates(): jax.lax.ppermute(heard, a_name, [(k, k ^ tick) for k in range(taken_in)])  13.3 us
    convert_element_type x3, other arithmetic, per_device(): rounded = rhs.astype(jnp.bfloat16)  10.9 us
    dot_general x3, matrix products, wall_solve(): jnp.einsum('ji,xik->xjk', synthesis, scaled, preferred_element_type=jnp.f...  10.4 us
    all_to_all x6, local copies, waits for them, and re-layouts, per_device(): lax.all_to_all(solved, 'gy', split_axis=1, concat_axis=2, tiled=True)  9 us
    ppermute x3, waiting for transfers between devices, extended(): lax.ppermute(tail, axis, [(i, (i + 1) % count) for i in range(count)])  8.82 us
  transfers between devices with their start and end apart: 15, of which 11 were waited for; matrix products, arithmetic and copies ran while one was open for 4% of the time, Pallas kernels for 0%

profile of v1, /device:TPU:0, one launch (start us, length us, event | category | flops | bytes accessed | tf_op | source)
XLA Modules:
  0.0 254.4 jit_solution(14871130868984471902)
XLA Ops:
  0.0 3.3 %collective-permute-start = (bf16[4,1,256,1024]{3,2,1,0:T(8,128)(2,1)}, bf16[4,1,256,1024]{3,2,1,0:T(8,128)(2,1)}, u32[]{:S(2)}, u32[]{:S(2)}) collective-permute-start(bf16[4,1,256,1024]{3,2,1,0:T(8,128)(2,1)} %param.8), channel_id=1, source_target_pairs={{4,0},{8,4},{12,8},{16,12},{20,16},{24,20},{28,24},{0,28},{5,1},{9... | collective-permute-start | bytes 6291464 | tf_op jit(solution)/shard_map/ppermute | solution.py:33
  3.3 0.7 constant_dynamic-slice_fusion.6
  4.0 44.7 %collective-permute-done = bf16[4,1,256,1024]{3,2,1,0:T(8,128)(2,1)} collective-permute-done((bf16[4,1,256,1024]{3,2,1,0:T(8,128)(2,1)}, bf16[4,1,256,1024]{3,2,1,0:T(8,128)(2,1)}, u32[]{:S(2)}, u32[]{:S(2)}) %collective-permute-start) | collective-permute-done | bytes 2097184 | tf_op jit(solution)/shard_map/ppermute | solution.py:33
  48.8 1.9 collective-permute-done.1
  50.7 5.7 %convert_add_fusion = (f32[4,1,256,1024]{3,2,1,0:T(8,128)S(1)}, f32[4,1,256,1024]{3,2,1,0:T(8,128)S(1)}) fusion(bf16[4,1,256,1024]{3,2,1,0:T(8,128)(2,1)} %param.9, bf16[4,1,256,1024]{3,2,1,0:T(8,128)(2,1)} %param.8, f32[256]{0:T(256)S(1)} %bitcast.143, bf16[4,1,256,1024]{3,2,1,0:T(8,128)(2,1)} %collective-permute-done.1, ...), kind=kLoop, calls=%fused_computation | loop fusion | flops 10485760 | bytes 16779264 | tf_op jit(solution)/shard_map/add | solution.py:85
  56.4 2.8 %fusion.29 = bf16[1,1,256,1024]{3,2,1,0:T(8,128)(2,1)S(1)} fusion(f32[4,1,256,1024]{3,2,1,0:T(8,128)S(1)} %get-tuple-element.6, f32[4,1,256,1024]{3,2,1,0:T(8,128)S(1)} %get-tuple-element.5, bf16[4,1,256,1024]{3,2,1,0:T(8,128)(2,1)} %param.9, bf16[4,1,256,1024]{3,2,1,0:T(8,128)(2,1)} %param.8), kind=kLoop, calls=%fused_computation.42 | loop fusion | flops 4194304 | bytes 6815744 | tf_op jit(solution)/shard_map/convert_element_type | solution.py:99
  59.2 0.1 dynamic-slice_bitcast_fusion
  59.3 0.4 copy-done.2
  59.7 1.6 collective-permute-start.2
  61.2 0.8 dynamic_slice.51
  62.0 2.6 %collective-permute-start.3 = (bf16[1,256,256]{2,1,0:T(8,128)(2,1)S(1)}, bf16[1,256,256]{2,1,0:T(8,128)(2,1)S(1)}, u32[]{:S(2)}, u32[]{:S(2)}) collective-permute-start(bf16[1,256,256]{2,1,0:T(8,128)(2,1)S(1)} %get-tuple-element.14), channel_id=1, source_target_pairs={{0,2},{1,3},{2,0},{3,1},{4,6},{5,7},{6,4},{7,5},{8,10},{9,11},{10,... | collective-permute-start | bytes 393224 | tf_op jit(solution)/shard_map/ppermute | solution.py:19
  64.6 0.2 collective-permute-start.4
  64.8 0.8 broadcast.367.clone.1
  65.6 0.7 bitcast_dynamic-update-slice_fusion.11
  66.3 0.7 bitcast_dynamic-update-slice_fusion.10
  67.0 5.4 %collective-permute-done.3 = bf16[1,256,256]{2,1,0:T(8,128)(2,1)S(1)} collective-permute-done((bf16[1,256,256]{2,1,0:T(8,128)(2,1)S(1)}, bf16[1,256,256]{2,1,0:T(8,128)(2,1)S(1)}, u32[]{:S(2)}, u32[]{:S(2)}) %collective-permute-start.3) | collective-permute-done | bytes 131104 | tf_op jit(solution)/shard_map/ppermute | solution.py:19
  72.3 0.7 bitcast_dynamic-update-slice_fusion.9
  73.0 0.7 bitcast_dynamic-update-slice_fusion.8
  73.7 3.2 %convolution_bitcast_fusion.4 = f32[1,1024,256]{1,2,0:T(8,128)S(1)} fusion(bf16[1024,1024]{1,0:T(8,128)(2,1)S(1)} %copy-done, bf16[1024,256]{1,0:T(8,128)(2,1)} %bitcast_dynamic-update-slice_fusion.8, bf16[1024,1024]{1,0:T(8,128)(2,1)} %param.14, f32[256]{0:T(256)S(1)} %dynamic_slice.51, f32[1024]{0:T(1024)S(1)} %copy-done.3), kind=kOutput, calls=%fused_computation.8 | convolution fusion | flops 1075314688 | bytes 5772288 | tf_op jit(solution)/shard_map/ji,xik->xjk/dot_general | solution.py:71
  76.9 1.9 copy.14
  78.8 27.0 %all_to_all.54 = f32[1,1024,256]{2,0,1:T(1,128)S(1)} all-to-all(f32[1,1024,256]{2,0,1:T(1,128)} %copy.14), channel_id=1, replica_groups=mesh['gx'=8,'gy'=4] {'gy'}, dimensions={1} | all-to-all | bytes 2097152 | tf_op jit(solution)/shard_map/all_to_all | solution.py:102
  105.8 0.7 convert_element_type.184
  106.5 1.5 copy.16
  108.0 2.3 convert_element_type.185
  110.2 3.7 %collective-permute-start.5 = (bf16[1,1,256,1024]{3,2,1,0:T(8,128)(2,1)}, bf16[1,1,256,1024]{3,2,1,0:T(8,128)(2,1)}, u32[]{:S(2)}, u32[]{:S(2)}) collective-permute-start(bf16[1,1,256,1024]{3,2,1,0:T(8,128)(2,1)} %convert_element_type.185), channel_id=1, source_target_pairs={{4,0},{8,4},{12,8},{16,12},{20,16},{24,20},{28,24},{0,28},{5,1},{9... | collective-permute-start | bytes 1572872 | tf_op jit(solution)/shard_map/ppermute | solution.py:33
  113.9 1.6 copy.15
  115.6 1.8 all_to_all.42
  117.3 7.4 %collective-permute-done.5 = bf16[1,1,256,1024]{3,2,1,0:T(8,128)(2,1)} collective-permute-done((bf16[1,1,256,1024]{3,2,1,0:T(8,128)(2,1)}, bf16[1,1,256,1024]{3,2,1,0:T(8,128)(2,1)}, u32[]{:S(2)}, u32[]{:S(2)}) %collective-permute-start.5) | collective-permute-done | bytes 524320 | tf_op jit(solution)/shard_map/ppermute | solution.py:33
  124.8 4.0 %collective-permute-done.6 = bf16[1,1,256,1024]{3,2,1,0:T(8,128)(2,1)} collective-permute-done((bf16[1,1,256,1024]{3,2,1,0:T(8,128)(2,1)}, bf16[1,1,256,1024]{3,2,1,0:T(8,128)(2,1)}, u32[]{:S(2)}, u32[]{:S(2)}) %collective-permute-start.6) | collective-permute-done | bytes 524320 | tf_op jit(solution)/shard_map/ppermute | solution.py:31
  128.8 4.1 %fusion.24 = bf16[1,256,1024]{2,1,0:T(8,128)(2,1)S(1)} fusion(f32[1,256,1024]{2,1,0:T(8,128)S(1)} %all_to_all.42, f32[4,1,256,1024]{3,2,1,0:T(8,128)} %copy-done.2, bf16[1,1,256,1024]{3,2,1,0:T(8,128)(2,1)} %convert_element_type.185, bf16[1,1,256,1024]{3,2,1,0:T(8,128)(2,1)} %collective-permute-done.6, bf16[1,1,256,1024]{3,2,1,0:T(8,128)(2,1)} %collective-permute-done.5, ...), kind=kLoop, calls=%fused_computation.36 | loop fusion | flops 6029312 | bytes 8914944 | tf_op jit(solution)/shard_map/convert_element_type | solution.py:99
  132.9 0.1 constant_dynamic-slice_fusion.3
  132.9 0.3 collective-permute-start.7
  133.2 1.8 collective-permute-start.8
  135.0 2.4 collective-permute-start.9
  137.4 0.8 broadcast.367.clone
  138.2 0.7 bitcast_dynamic-update-slice_fusion.7
  138.9 0.5 collective-permute-done.7
  139.4 0.7 bitcast_dynamic-update-slice_fusion.6
  140.1 5.8 %collective-permute-done.8 = bf16[1,256,256]{2,1,0:T(8,128)(2,1)S(1)} collective-permute-done((bf16[1,256,256]{2,1,0:T(8,128)(2,1)S(1)}, bf16[1,256,256]{2,1,0:T(8,128)(2,1)S(1)}, u32[]{:S(2)}, u32[]{:S(2)}) %collective-permute-start.8) | collective-permute-done | bytes 131104 | tf_op jit(solution)/shard_map/ppermute | solution.py:19
  145.9 0.7 bitcast_dynamic-update-slice_fusion.5
  146.6 0.7 bitcast_dynamic-update-slice_fusion.4
  147.3 3.2 %convolution_bitcast_fusion.2 = f32[1,1024,256]{1,2,0:T(8,128)S(1)} fusion(bf16[1024,1024]{1,0:T(8,128)(2,1)S(1)} %copy-done, bf16[1024,256]{1,0:T(8,128)(2,1)} %bitcast_dynamic-update-slice_fusion.4, bf16[1024,1024]{1,0:T(8,128)(2,1)} %param.14, f32[256]{0:T(256)S(1)} %dynamic_slice.51, f32[1024]{0:T(1024)S(1)} %copy-done.3), kind=kOutput, calls=%fused_computation.6 | convolution fusion | flops 1075314688 | bytes 5772288 | tf_op jit(solution)/shard_map/ji,xik->xjk/dot_general | solution.py:71
  150.4 1.9 copy.17
  152.3 27.8 %all_to_all.55 = f32[1,1024,256]{2,0,1:T(1,128)S(1)} all-to-all(f32[1,1024,256]{2,0,1:T(1,128)} %copy.17), channel_id=1, replica_groups=mesh['gx'=8,'gy'=4] {'gy'}, dimensions={1} | all-to-all | bytes 2097152 | tf_op jit(solution)/shard_map/all_to_all | solution.py:102
  180.1 0.7 convert_element_type.192
  180.9 1.5 copy.19
  182.3 2.3 convert_element_type.193
  184.6 0.5 collective-permute-start.11
  185.1 1.6 copy.18
  186.7 1.8 all_to_all.46
  188.5 6.8 %collective-permute-done.10 = bf16[1,1,256,1024]{3,2,1,0:T(8,128)(2,1)} collective-permute-done((bf16[1,1,256,1024]{3,2,1,0:T(8,128)(2,1)}, bf16[1,1,256,1024]{3,2,1,0:T(8,128)(2,1)}, u32[]{:S(2)}, u32[]{:S(2)}) %collective-permute-start.10) | collective-permute-done | bytes 524320 | tf_op jit(solution)/shard_map/ppermute | solution.py:33
  195.3 2.9 %collective-permute-done.11 = bf16[1,1,256,1024]{3,2,1,0:T(8,128)(2,1)} collective-permute-done((bf16[1,1,256,1024]{3,2,1,0:T(8,128)(2,1)}, bf16[1,1,256,1024]{3,2,1,0:T(8,128)(2,1)}, u32[]{:S(2)}, u32[]{:S(2)}) %collective-permute-start.11) | collective-permute-done | bytes 524320 | tf_op jit(solution)/shard_map/ppermute | solution.py:31
  198.1 4.1 %fusion.18 = bf16[1,256,1024]{2,1,0:T(8,128)(2,1)S(1)} fusion(f32[1,256,1024]{2,1,0:T(8,128)S(1)} %all_to_all.46, f32[4,1,256,1024]{3,2,1,0:T(8,128)} %copy-done.2, bf16[1,1,256,1024]{3,2,1,0:T(8,128)(2,1)} %convert_element_type.193, bf16[1,1,256,1024]{3,2,1,0:T(8,128)(2,1)} %collective-permute-done.11, ...), kind=kLoop, calls=%fused_computation.29 | loop fusion | flops 6029312 | bytes 8914944 | tf_op jit(solution)/shard_map/convert_element_type | solution.py:99
  202.2 0.1 constant_dynamic-slice_fusion.2
  202.3 0.3 collective-permute-start.12
  202.5 1.8 collective-permute-start.13
  204.3 2.4 collective-permute-start.14
  206.8 3.1 %collective-permute-done.12 = bf16[1,256,256]{2,1,0:T(8,128)(2,1)S(1)} collective-permute-done((bf16[1,256,256]{2,1,0:T(8,128)(2,1)S(1)}, bf16[1,256,256]{2,1,0:T(8,128)(2,1)S(1)}, u32[]{:S(2)}, u32[]{:S(2)}) %collective-permute-start.12) | collective-permute-done | bytes 131104 | tf_op jit(solution)/shard_map/ppermute | solution.py:19
  209.9 5.5 %collective-permute-done.13 = bf16[1,256,256]{2,1,0:T(8,128)(2,1)S(1)} collective-permute-done((bf16[1,256,256]{2,1,0:T(8,128)(2,1)S(1)}, bf16[1,256,256]{2,1,0:T(8,128)(2,1)S(1)}, u32[]{:S(2)}, u32[]{:S(2)}) %collective-permute-start.13) | collective-permute-done | bytes 131104 | tf_op jit(solution)/shard_map/ppermute | solution.py:19
  215.5 4.0 %convolution_bitcast_fusion = f32[1,1024,256]{1,2,0:T(8,128)} fusion(bf16[1024,1024]{1,0:T(8,128)(2,1)S(1)} %copy-done, bf16[1024,256]{1,0:T(8,128)(2,1)S(1)} %bitcast_dynamic-update-slice_fusion, bf16[1024,1024]{1,0:T(8,128)(2,1)} %param.14, f32[256]{0:T(256)S(1)} %dynamic_slice.51, f32[1024]{0:T(1024)S(1)} %copy-done.3), kind=kOutput, calls=%fused_computation.4 | convolution fusion | flops 1075314688 | bytes 5772288 | tf_op jit(solution)/shard_map/ji,xik->xjk/dot_general | solution.py:71
  219.5 2.4 copy.20
  221.9 30.3 %all_to_all.56 = f32[1,1024,256]{2,0,1:T(1,128)S(1)} all-to-all(f32[1,1024,256]{2,0,1:T(1,128)S(1)} %copy.20), channel_id=1, replica_groups=mesh['gx'=8,'gy'=4] {'gy'}, dimensions={1} | all-to-all | bytes 2097152 | tf_op jit(solution)/shard_map/all_to_all | solution.py:102
  252.3 0.7 copy.21
  252.9 1.5 all_to_all.50
  (19 shorter events, 0.1 us)
Async XLA Ops:
  0.0 73.7 %copy-start = (bf16[1024,1024]{1,0:T(8,128)(2,1)S(1)}, bf16[1024,1024]{1,0:T(8,128)(2,1)}, u32[]{:S(2)}) copy-start(bf16[1024,1024]{1,0:T(8,128)(2,1)} %param.15) | copy-start | bytes 6291460
  0.0 48.8 %collective-permute-start = (bf16[4,1,256,1024]{3,2,1,0:T(8,128)(2,1)}, bf16[4,1,256,1024]{3,2,1,0:T(8,128)(2,1)}, u32[]{:S(2)}, u32[]{:S(2)}) collective-permute-start(bf16[4,1,256,1024]{3,2,1,0:T(8,128)(2,1)} %param.8), channel_id=1, source_target_pairs={{4,0},{8,4},{12,8},{16,12},{20,16},{24,20},{28,24},{0,28},{5,1},{9... | collective-permute-start | bytes 6291464 | tf_op jit(solution)/shard_map/ppermute | solution.py:33
  3.3 47.4 %collective-permute-start.1 = (bf16[4,1,256,1024]{3,2,1,0:T(8,128)(2,1)}, bf16[4,1,256,1024]{3,2,1,0:T(8,128)(2,1)}, u32[]{:S(2)}, u32[]{:S(2)}) collective-permute-start(bf16[4,1,256,1024]{3,2,1,0:T(8,128)(2,1)} %param.8), channel_id=1, source_target_pairs={{0,4},{4,8},{8,12},{12,16},{16,20},{20,24},{24,28},{28,0},{1,5},{5... | collective-permute-start | bytes 6291464 | tf_op jit(solution)/shard_map/ppermute | solution.py:31
  56.4 2.8 %copy-start.1 = (f32[4,1,256,1024]{3,2,1,0:T(8,128)}, f32[4,1,256,1024]{3,2,1,0:T(8,128)S(1)}, u32[]{:S(2)}) copy-start(f32[4,1,256,1024]{3,2,1,0:T(8,128)S(1)} %get-tuple-element.5) | copy-start | bytes 12582916
  56.4 3.3 %copy-start.2 = (f32[4,1,256,1024]{3,2,1,0:T(8,128)}, f32[4,1,256,1024]{3,2,1,0:T(8,128)S(1)}, u32[]{:S(2)}) copy-start(f32[4,1,256,1024]{3,2,1,0:T(8,128)S(1)} %get-tuple-element.6) | copy-start | bytes 12582916
  59.2 14.5 %copy-start.3 = (f32[1024]{0:T(1024)S(1)}, f32[1024]{0:T(1024)}, u32[]{:S(2)}) copy-start(f32[1024]{0:T(1024)} %param.12) | copy-start | bytes 12292
  59.7 6.7 %collective-permute-start.2 = (bf16[1,256,256]{2,1,0:T(8,128)(2,1)S(1)}, bf16[1,256,256]{2,1,0:T(8,128)(2,1)S(1)}, u32[]{:S(2)}, u32[]{:S(2)}) collective-permute-start(bf16[1,256,256]{2,1,0:T(8,128)(2,1)S(1)} %get-tuple-element.15), channel_id=1, source_target_pairs={{0,1},{1,0},{2,3},{3,2},{4,5},{5,4},{6,7},{7,6},{8,9},{9,8},{10,11... | collective-permute-start | bytes 393224 | tf_op jit(solution)/shard_map/ppermute | solution.py:19
  62.0 10.4 %collective-permute-start.3 = (bf16[1,256,256]{2,1,0:T(8,128)(2,1)S(1)}, bf16[1,256,256]{2,1,0:T(8,128)(2,1)S(1)}, u32[]{:S(2)}, u32[]{:S(2)}) collective-permute-start(bf16[1,256,256]{2,1,0:T(8,128)(2,1)S(1)} %get-tuple-element.14), channel_id=1, source_target_pairs={{0,2},{1,3},{2,0},{3,1},{4,6},{5,7},{6,4},{7,5},{8,10},{9,11},{10,... | collective-permute-start | bytes 393224 | tf_op jit(solution)/shard_map/ppermute | solution.py:19
  64.6 8.4 %collective-permute-start.4 = (bf16[1,256,256]{2,1,0:T(8,128)(2,1)S(1)}, bf16[1,256,256]{2,1,0:T(8,128)(2,1)S(1)}, u32[]{:S(2)}, u32[]{:S(2)}) collective-permute-start(bf16[1,256,256]{2,1,0:T(8,128)(2,1)S(1)} %get-tuple-element.13), channel_id=1, source_target_pairs={{0,3},{1,2},{2,1},{3,0},{4,7},{5,6},{6,5},{7,4},{8,11},{9,10},{10,... | collective-permute-start | bytes 393224 | tf_op jit(solution)/shard_map/ppermute | solution.py:19
  110.2 14.5 %collective-permute-start.5 = (bf16[1,1,256,1024]{3,2,1,0:T(8,128)(2,1)}, bf16[1,1,256,1024]{3,2,1,0:T(8,128)(2,1)}, u32[]{:S(2)}, u32[]{:S(2)}) collective-permute-start(bf16[1,1,256,1024]{3,2,1,0:T(8,128)(2,1)} %convert_element_type.185), channel_id=1, source_target_pairs={{4,0},{8,4},{12,8},{16,12},{20,16},{24,20},{28,24},{0,28},{5,1},{9... | collective-permute-start | bytes 1572872 | tf_op jit(solution)/shard_map/ppermute | solution.py:33
  113.9 14.9 %collective-permute-start.6 = (bf16[1,1,256,1024]{3,2,1,0:T(8,128)(2,1)}, bf16[1,1,256,1024]{3,2,1,0:T(8,128)(2,1)}, u32[]{:S(2)}, u32[]{:S(2)}) collective-permute-start(bf16[1,1,256,1024]{3,2,1,0:T(8,128)(2,1)} %convert_element_type.185), channel_id=1, source_target_pairs={{0,4},{4,8},{8,12},{12,16},{16,20},{20,24},{24,28},{28,0},{1,5},{5... | collective-permute-start | bytes 1572872 | tf_op jit(solution)/shard_map/ppermute | solution.py:31
  132.9 6.5 %collective-permute-start.7 = (bf16[1,256,256]{2,1,0:T(8,128)(2,1)S(1)}, bf16[1,256,256]{2,1,0:T(8,128)(2,1)S(1)}, u32[]{:S(2)}, u32[]{:S(2)}) collective-permute-start(bf16[1,256,256]{2,1,0:T(8,128)(2,1)S(1)} %get-tuple-element.12), channel_id=1, source_target_pairs={{0,1},{1,0},{2,3},{3,2},{4,5},{5,4},{6,7},{7,6},{8,9},{9,8},{10,11... | collective-permute-start | bytes 393224 | tf_op jit(solution)/shard_map/ppermute | solution.py:19
  133.2 12.7 %collective-permute-start.8 = (bf16[1,256,256]{2,1,0:T(8,128)(2,1)S(1)}, bf16[1,256,256]{2,1,0:T(8,128)(2,1)S(1)}, u32[]{:S(2)}, u32[]{:S(2)}) collective-permute-start(bf16[1,256,256]{2,1,0:T(8,128)(2,1)S(1)} %get-tuple-element.11), channel_id=1, source_target_pairs={{0,2},{1,3},{2,0},{3,1},{4,6},{5,7},{6,4},{7,5},{8,10},{9,11},{10,... | collective-permute-start | bytes 393224 | tf_op jit(solution)/shard_map/ppermute | solution.py:19
  135.0 11.6 %collective-permute-start.9 = (bf16[1,256,256]{2,1,0:T(8,128)(2,1)S(1)}, bf16[1,256,256]{2,1,0:T(8,128)(2,1)S(1)}, u32[]{:S(2)}, u32[]{:S(2)}) collective-permute-start(bf16[1,256,256]{2,1,0:T(8,128)(2,1)S(1)} %get-tuple-element.10), channel_id=1, source_target_pairs={{0,3},{1,2},{2,1},{3,0},{4,7},{5,6},{6,5},{7,4},{8,11},{9,10},{10,... | collective-permute-start | bytes 393224 | tf_op jit(solution)/shard_map/ppermute | solution.py:19
  184.6 10.7 %collective-permute-start.10 = (bf16[1,1,256,1024]{3,2,1,0:T(8,128)(2,1)}, bf16[1,1,256,1024]{3,2,1,0:T(8,128)(2,1)}, u32[]{:S(2)}, u32[]{:S(2)}) collective-permute-start(bf16[1,1,256,1024]{3,2,1,0:T(8,128)(2,1)} %convert_element_type.193), channel_id=1, source_target_pairs={{4,0},{8,4},{12,8},{16,12},{20,16},{24,20},{28,24},{0,28},{5,1},{9... | collective-permute-start | bytes 1572872 | tf_op jit(solution)/shard_map/ppermute | solution.py:33
  184.6 13.5 %collective-permute-start.11 = (bf16[1,1,256,1024]{3,2,1,0:T(8,128)(2,1)}, bf16[1,1,256,1024]{3,2,1,0:T(8,128)(2,1)}, u32[]{:S(2)}, u32[]{:S(2)}) collective-permute-start(bf16[1,1,256,1024]{3,2,1,0:T(8,128)(2,1)} %convert_element_type.193), channel_id=1, source_target_pairs={{0,4},{4,8},{8,12},{12,16},{16,20},{20,24},{24,28},{28,0},{1,5},{5... | collective-permute-start | bytes 1572872 | tf_op jit(solution)/shard_map/ppermute | solution.py:31
  202.3 7.7 %collective-permute-start.12 = (bf16[1,256,256]{2,1,0:T(8,128)(2,1)S(1)}, bf16[1,256,256]{2,1,0:T(8,128)(2,1)S(1)}, u32[]{:S(2)}, u32[]{:S(2)}) collective-permute-start(bf16[1,256,256]{2,1,0:T(8,128)(2,1)S(1)} %get-tuple-element.9), channel_id=1, source_target_pairs={{0,1},{1,0},{2,3},{3,2},{4,5},{5,4},{6,7},{7,6},{8,9},{9,8},{10,11... | collective-permute-start | bytes 393224 | tf_op jit(solution)/shard_map/ppermute | solution.py:19
  202.5 12.9 %collective-permute-start.13 = (bf16[1,256,256]{2,1,0:T(8,128)(2,1)S(1)}, bf16[1,256,256]{2,1,0:T(8,128)(2,1)S(1)}, u32[]{:S(2)}, u32[]{:S(2)}) collective-permute-start(bf16[1,256,256]{2,1,0:T(8,128)(2,1)S(1)} %get-tuple-element.8), channel_id=1, source_target_pairs={{0,2},{1,3},{2,0},{3,1},{4,6},{5,7},{6,4},{7,5},{8,10},{9,11},{10,... | collective-permute-start | bytes 393224 | tf_op jit(solution)/shard_map/ppermute | solution.py:19
  204.3 11.2 %collective-permute-start.14 = (bf16[1,256,256]{2,1,0:T(8,128)(2,1)S(1)}, bf16[1,256,256]{2,1,0:T(8,128)(2,1)S(1)}, u32[]{:S(2)}, u32[]{:S(2)}) collective-permute-start(bf16[1,256,256]{2,1,0:T(8,128)(2,1)S(1)} %get-tuple-element.7), channel_id=1, source_target_pairs={{0,3},{1,2},{2,1},{3,0},{4,7},{5,6},{6,5},{7,4},{8,11},{9,10},{10,... | collective-permute-start | bytes 393224 | tf_op jit(solution)/shard_map/ppermute | solution.py:19
